TPU v7x, 512 devices: a whole 4x4x16 slice. The times are simulated.
512 devices in a mesh: tensor: 4 (over z_hi, core), row: 8 (over z_lo), col: 16 (over x, y).
Axes of the slice: x: 4, y: 4, z: 16 (z_hi: 2, z_lo: 8; z = z_hi * 8 + z_lo), core: 2. Of those that a mesh axis runs over, the one named last changes fastest.
Arguments:
- features: bfloat16 [16384, 6144], P(('row', 'col'), 'tensor'), may hold values from -8 to 8
- w_proj: bfloat16 [6144, 1024], P('tensor'), may hold values from -0.078125 to 0.078125
- flags: int32 [16384], P(('row', 'col')), may hold values 0 or 1
- rates: float32 [5], replicated, may hold values from 0.25 to 4
Outputs:
- feature_grad: bfloat16 [16384, 6144], P(('row', 'col'), 'tensor')
All inputs are finite; a program needn't handle non-finite values. No bound on the sum of `flags` on one device may be relied on, other than what follows from the above.
Results may differ from a plain program's by a relative error of at most 0.029.
Values may be sent and summed in bfloat16 or wider, within the bound.
No kernel may reach another device: no remote copies, remote signals or barrier semaphores. Data moves between devices by JAX's collectives and lax.ppermute only.
A program may use at most 64 MiB of HBM per device.

v0:
```python
import jax
import jax.numpy as jnp
from jax import lax
from jax.sharding import PartitionSpec as P


def tensor_sum(value):
    return lax.psum(value.astype(jnp.bfloat16), "tensor").astype(jnp.float32)


def shards(features, w_proj, flags, rates):
    group = features.shape[0]
    width = w_proj.shape[1]
    n_tensor = lax.axis_size("tensor")
    quarter = group // n_tensor
    tpos = lax.axis_index("tensor")
    signs = (1 - 2 * flags).astype(jnp.bfloat16)
    own_s = lax.dynamic_slice_in_dim(signs, tpos * quarter, quarter, 0)
    proj_full = tensor_sum(jnp.dot(features, w_proj, preferred_element_type=jnp.float32)).astype(
        jnp.bfloat16
    )
    own_z = lax.dynamic_slice_in_dim(proj_full, tpos * quarter, quarter, 0)
    row_z, row_s = (
        lax.all_gather(proj_full, "row", axis=0, tiled=True),
        lax.all_gather(signs, "row", axis=0, tiled=True),
    )
    col_z, col_s = (
        lax.all_gather(own_z, "col", axis=0, tiled=True),
        lax.all_gather(own_s, "col", axis=0, tiled=True),
    )
    row_norm = jnp.sum(jnp.square(row_z.astype(jnp.float32)), axis=1)
    col_norm = jnp.sum(jnp.square(col_z.astype(jnp.float32)), axis=1)
    cross = lax.dot_general(
        row_z, col_z, (((1,), (1,)), ((), ())), preferred_element_type=jnp.float32
    )
    dist = jnp.maximum(row_norm[:, None] + col_norm[None, :] - 2.0 * cross, 0.0) / width
    kernel = jnp.zeros_like(dist)
    for band in range(rates.shape[0]):
        kernel = kernel + rates[band] * jnp.exp(-rates[band] * dist)
    mixed = (
        -16.0
        / width
        * row_s.astype(jnp.float32)[:, None]
        * col_s.astype(jnp.float32)[None, :]
        * kernel
    )
    rounded = mixed.astype(jnp.bfloat16)
    row_total = jnp.sum(mixed, axis=1)
    col_total = jnp.sum(mixed, axis=0)
    block = rounded
    lead = col_total
    own_rows = col_z
    other = lax.dot_general(
        block, row_z, (((0,), (0,)), ((), ())), preferred_element_type=jnp.float32
    )
    col_part = lax.psum_scatter(
        (lead[:, None] * own_rows.astype(jnp.float32) - other).astype(jnp.bfloat16),
        "col",
        scatter_dimension=0,
        tiled=True,
    ).astype(jnp.float32)
    block = rounded
    lead = row_total
    own_rows = row_z
    row_part = lax.psum_scatter(
        (
            lead[:, None] * own_rows.astype(jnp.float32)
            - jnp.dot(block, col_z, preferred_element_type=jnp.float32)
        ).astype(jnp.bfloat16),
        "row",
        scatter_dimension=0,
        tiled=True,
    ).astype(jnp.float32)
    placed = lax.dynamic_update_slice_in_dim(
        jnp.zeros((group, width), jnp.float32), col_part, tpos * quarter, 0
    )
    grad_z = tensor_sum(row_part + placed).astype(jnp.bfloat16)
    result = lax.dot_general(
        grad_z, w_proj, (((1,), (1,)), ((), ())), preferred_element_type=jnp.float32
    )
    return result.astype(jnp.bfloat16)


def solution(mesh):
    in_specs = (P(("row", "col"), "tensor"), P("tensor", None), P(("row", "col")), P())
    out_specs = P(("row", "col"), "tensor")
    return jax.shard_map(shards, mesh=mesh, in_specs=in_specs, out_specs=out_specs, check_vma=False)
```

profile of v0, /device:TPU:1, one launch (start us, length us, event | category | flops | bytes accessed | tf_op | source)
XLA Modules:
  0.0 494.9 jit_solution(233492675417268353)
XLA Ops:
  6.5 0.0 copy-start
  6.5 0.0 copy-start.4
  6.5 0.0 copy-start.3
  6.5 0.0 all-reduce.4.cloned.1.call-start
  6.5 1.9 copy-done
  8.4 2.3 convolution_convert_fusion.1
  10.7 0.0 all-reduce.4.cloned.1.call-update
  10.7 0.0 all-gather.6.cloned.1.call-start
  10.8 90.4 %all-reduce.4.cloned.1.call-done = bf16[128,1024]{1,0:T(8,128)(2,1)} async-done(((bf16[128,1024]{1,0:T(8,128)(2,1)}), bf16[128,1024]{1,0:T(8,128)(2,1)}) %all-reduce.4.cloned.1.call-update) | async-done | bytes 262160 | tf_op jit(solution)/shard_map/psum | solution.py:8
  101.2 1.5 constant_dynamic-slice_fusion
  102.7 0.0 all-gather.6.cloned.1.call-update
  102.7 0.0 all-gather.4.cloned.1.call-start
  102.7 0.7 all-gather.4.cloned.1.call-update
  103.4 0.0 reduce-scatter.3.cloned.1.call-start
  103.5 0.0 copy-done.4
  103.5 0.1 dynamic_slice.6
  103.6 1.3 dynamic-slice.1
  105.5 0.2 dynamic-update-slice.1
  105.7 31.4 %all-reduce = bf16[512]{0:T(512)(128)(2,1)S(1)} all-reduce(bf16[512]{0:T(512)(128)(2,1)S(1)} %dynamic-update-slice.1), channel_id=1, replica_groups=mesh['tensor'=4,'row'=8,'col'=16] {'col'}, use_global_device_ids=true, to_apply=%add | all-reduce | flops 512 | bytes 2048
  137.1 0.0 copy-done.3
  137.1 0.7 fusion.10
  140.9 22.1 %all-gather = bf16[8,1,128]{2,1,0:T(2,128)(2,1)S(1)} all-gather(bf16[1,1,128]{2,1,0:T(2,128)(2,1)S(1)} %get-tuple-element.7), channel_id=1, replica_groups=mesh['tensor'=4,'row'=8,'col'=16] {'row'}, dimensions={0}, use_global_device_ids=true | all-gather | bytes 2304 | tf_op jit(solution)/shard_map/all_gather | solution.py:25
  163.0 0.0 all-gather.6.cloned.1.call-done
  163.1 1.5 fusion.3
  164.6 55.9 %all-gather.4.cloned.1.call-done = bf16[1024,1024]{1,0:T(8,128)(2,1)} async-done(((bf16[128,1024]{1,0:T(8,128)(2,1)}), bf16[1024,1024]{1,0:T(8,128)(2,1)}) %all-gather.4.cloned.1.call-update) | async-done | bytes 2097168 | tf_op jit(solution)/shard_map/all_gather | solution.py:24
  220.5 0.0 copy-start.1
  220.5 2.2 fusion
  222.7 0.0 copy-done.1
  222.7 0.0 copy-start.2
  222.7 8.2 %fusion.9 = (f32[512]{0:T(512)S(1)}, f32[1024]{0:T(1024)S(1)}, bf16[1024,512]{1,0:T(8,128)(2,1)S(1)}) fusion(f32[]{:T(128)S(6)} %mul.157, f32[]{:T(128)} %bitcast.7, f32[]{:T(128)S(6)} %mul.152, f32[]{:T(128)} %bitcast.6, f32[]{:T(128)S(6)} %mul.147, f32[]{:T(128)} %bitcast.5, f32[]{:T(128)S(6)} %mul.142, f32[]{:T(128)} %bitcast.4, f32[]{:T(128)S(6)} %mul.137, ...), kind=kOutput, calls=%fused_computation.20 | convolution fusion | flops 1085798912 | bytes 4212776 | tf_op jit(solution)/shard_map/dot_general | solution.py:33
  230.9 0.0 copy-start.5
  230.9 1.0 copy-done.5
  231.9 0.0 copy-done.2
  231.9 2.6 fusion.2
  234.5 0.0 reduce-scatter.3.cloned.1.call-update
  234.5 0.0 reduce-scatter.5.cloned.1.call-start
  234.5 4.5 fusion.5
  239.0 0.0 reduce-scatter.5.cloned.1.call-update
  239.0 0.0 all-reduce.6.cloned.1.call-start
  239.1 64.8 %reduce-scatter.3.cloned.1.call-done = bf16[128,1024]{1,0:T(8,128)(2,1)} async-done(((bf16[1024,1024]{1,0:T(8,128)(2,1)}), bf16[128,1024]{1,0:T(8,128)(2,1)}) %reduce-scatter.3.cloned.1.call-update) | async-done | bytes 262160 | tf_op jit(solution)/shard_map/reduce_scatter | solution.py:65
  303.9 1.8 convert_element_type.55
  305.7 89.9 %reduce-scatter.5.cloned.1.call-done = bf16[32,1024]{1,0:T(8,128)(2,1)} async-done(((bf16[512,1024]{1,0:T(8,128)(2,1)}), bf16[32,1024]{1,0:T(8,128)(2,1)}) %reduce-scatter.5.cloned.1.call-update) | async-done | bytes 65552 | tf_op jit(solution)/shard_map/reduce_scatter | solution.py:56
  395.5 1.6 add_dynamic-update-slice_fusion
  397.1 1.8 convert_element_type.59
  398.9 0.0 all-reduce.6.cloned.1.call-update
  398.9 86.3 %all-reduce.6.cloned.1.call-done = bf16[128,1024]{1,0:T(8,128)(2,1)} async-done(((bf16[128,1024]{1,0:T(8,128)(2,1)}), bf16[128,1024]{1,0:T(8,128)(2,1)}) %all-reduce.6.cloned.1.call-update) | async-done | bytes 262160 | tf_op jit(solution)/shard_map/psum | solution.py:8
  485.2 2.9 convolution_convert_fusion
  (4 shorter events, 0.0 us)
Async XLA Ops:
  6.5 1.9 copy-start
  6.5 96.9 %copy-start.4 = (s32[128]{0:T(128)S(1)}, s32[128]{0:T(128)}, u32[]{:S(2)}) copy-start(s32[128]{0:T(128)} %param.6) | copy-start | bytes 1540
  6.5 130.6 %copy-start.3 = (f32[5]{0:T(128)S(1)}, f32[5]{0:T(128)}, u32[]{:S(2)}) copy-start(f32[5]{0:T(128)} %param.7) | copy-start | bytes 64
  6.5 94.7 %all-reduce.4.cloned.1.call-start = ((), (), s32[]{:S(2)}) async-start(), calls=%async_computation.2 | async-start | bytes 524288 | tf_op jit(solution)/shard_map/psum | solution.py:8
  10.7 152.3 %all-gather.6.cloned.1.call-start = ((), (), s32[]{:S(2)}) async-start(), calls=%async_computation.4 | async-start | bytes 1114112 | tf_op jit(solution)/shard_map/all_gather | solution.py:28
  102.7 117.8 %all-gather.4.cloned.1.call-start = ((), (), s32[]{:S(2)}) async-start(), calls=%async_computation.3 | async-start | bytes 2359296 | tf_op jit(solution)/shard_map/all_gather | solution.py:24
  103.4 200.4 %reduce-scatter.3.cloned.1.call-start = ((), (), s32[]{:S(2)}) async-start(), calls=%async_computation.5 | async-start | bytes 2359296 | tf_op jit(solution)/shard_map/reduce_scatter | solution.py:65
  220.5 2.2 copy-start.1
  222.7 9.2 %copy-start.2 = (bf16[512,1024]{1,0:T(8,128)(2,1)S(1)}, bf16[512,1024]{1,0:T(8,128)(2,1)}, u32[]{:S(2)}) copy-start(bf16[512,1024]{1,0:T(8,128)(2,1)} %all-gather.6.cloned.1.call-done) | copy-start | bytes 3145732
  230.9 1.0 copy-start.5
  234.5 161.1 %reduce-scatter.5.cloned.1.call-start = ((), (), s32[]{:S(2)}) async-start(), calls=%async_computation.6 | async-start | bytes 1114112 | tf_op jit(solution)/shard_map/reduce_scatter | solution.py:56
  239.0 246.2 %all-reduce.6.cloned.1.call-start = ((), (), s32[]{:S(2)}) async-start(), calls=%async_computation.7 | async-start | bytes 524288 | tf_op jit(solution)/shard_map/psum | solution.py:8
Sparse Core Ops, SparseCore 0:
  10.9 90.2 all-reduce.3
  104.6 46.9 all-gather.5
  153.9 66.4 all-gather.3
  234.6 69.2 reduce-scatter.2
  308.3 87.1 reduce-scatter.4
  399.0 86.0 all-reduce.5
where the time goes:
time: 495 us
  waiting for transfers between devices  388 us (78%)
  blocking collectives  53.5 us (11%)
  matrix products  20.4 us (4%)
  between operations  17.3 us (3%)
  other arithmetic  8.87 us (2%)
  local copies, waits for them, and re-layouts  6.63 us (1%)
    psum x2, waiting for transfers between devices, tensor_sum(): return lax.psum(value.astype(jnp.bfloat16), 'tensor').astype(jnp.float32)  177 us
    reduce_scatter x1, waiting for transfers between devices, shards(): lax.psum_scatter((lead[:, None] * own_rows.astype(jnp.float32) - other).a...  89.9 us
    reduce_scatter x1, waiting for transfers between devices, shards(): lax.psum_scatter((lead[:, None] * own_rows.astype(jnp.float32) - jnp.dot(...  64.8 us
    all_gather x1, waiting for transfers between devices, shards(): lax.all_gather(proj_full, 'row', axis=0, tiled=True)  55.9 us
    unnamed x1, blocking collectives  31.4 us
    all_gather x1, blocking collectives, shards(): lax.all_gather(signs, 'row', axis=0, tiled=True)  22.1 us
  transfers between devices with their start and end apart: 6, of which 5 were waited for; matrix products, arithmetic and copies ran while one was open for 2% of the time, Pallas kernels for 0%

commit v1 on v0

--- a/solution.py
+++ b/solution.py
@@ -5,7 +5,7 @@
 
 
 def tensor_sum(value):
-    return lax.psum(value.astype(jnp.bfloat16), "tensor").astype(jnp.float32)
+    return jnp.sum(lax.all_gather(value.astype(jnp.bfloat16), "tensor"), axis=0).astype(jnp.float32)
 
 
 def shards(features, w_proj, flags, rates):

time: 495 us -> 433 us (0.87)
  waiting for transfers between devices: 388 us -> 324 us
    psum x2 -> x0, waiting for transfers between devices: 177 us -> none  [tensor_sum(): return lax.psum(value.astype(jnp.bfloat16), 'tensor').astype(jnp.float32)]
    all_gather x0 -> x2, waiting for transfers between devices: none -> 114 us  [tensor_sum(): lax.all_gather(value.astype(jnp.bfloat16), 'tensor')]
where the time goes in v1:
time: 433 us; the launch traced here: 432 us
  waiting for transfers between devices  324 us (75%)
  blocking collectives  53.8 us (12%)
  matrix products  19.5 us (5%)
  between operations  17.3 us (4%)
  other arithmetic  11.7 us (3%)
  local copies, waits for them, and re-layouts  5.84 us (1%)
    all_gather x2, waiting for transfers between devices, tensor_sum(): lax.all_gather(value.astype(jnp.bfloat16), 'tensor')  114 us
    reduce_scatter x1, waiting for transfers between devices, shards(): lax.psum_scatter((lead[:, None] * own_rows.astype(jnp.float32) - other).a...  89.8 us
    reduce_scatter x1, waiting for transfers between devices, shards(): lax.psum_scatter((lead[:, None] * own_rows.astype(jnp.float32) - jnp.dot(...  64.8 us
    all_gather x1, waiting for transfers between devices, shards(): lax.all_gather(proj_full, 'row', axis=0, tiled=True)  54.9 us
    unnamed x1, blocking collectives  33.3 us
    all_gather x1, blocking collectives, shards(): lax.all_gather(signs, 'row', axis=0, tiled=True)  20.5 us
  transfers between devices with their start and end apart: 6, of which 5 were waited for; matrix products, arithmetic and copies ran while one was open for 2% of the time, Pallas kernels for 0%

profile of v1, /device:TPU:1, one launch (start us, length us, event | category | flops | bytes accessed | tf_op | source)
XLA Modules:
  0.0 432.2 jit_solution(1959949821919307215)
XLA Ops:
  6.5 0.0 copy-start
  6.5 0.0 all-gather.12.cloned.1.call-start
  6.5 1.9 copy-done
  8.4 2.3 convolution_convert_fusion.1
  10.7 0.0 all-gather.12.cloned.1.call-update
  10.7 0.0 all-gather.10.cloned.1.call-start
  10.8 58.9 %all-gather.12.cloned.1.call-done = bf16[512,1024]{1,0:T(8,128)(2,1)} async-done(((bf16[128,1024]{1,0:T(8,128)(2,1)}), bf16[512,1024]{1,0:T(8,128)(2,1)}) %all-gather.12.cloned.1.call-update) | async-done | bytes 1048592 | tf_op jit(solution)/shard_map/all_gather | solution.py:8
  69.7 1.4 reduce_sum.60
  71.2 0.0 copy-start.2
  71.2 0.7 constant_dynamic-slice_fusion
  71.9 0.0 all-gather.10.cloned.1.call-update
  71.9 0.0 all-gather.8.cloned.1.call-start
  71.9 0.0 copy-done.2
  72.0 0.7 all-gather.8.cloned.1.call-update
  72.6 0.0 reduce-scatter.3.cloned.1.call-start
  72.7 0.0 copy-done.5
  72.7 0.1 dynamic_slice.6
  72.8 1.3 dynamic-slice.1
  74.6 0.2 dynamic-update-slice.1
  74.9 33.3 %all-reduce = bf16[512]{0:T(512)(128)(2,1)S(1)} all-reduce(bf16[512]{0:T(512)(128)(2,1)S(1)} %dynamic-update-slice.1), channel_id=1, replica_groups=mesh['tensor'=4,'row'=8,'col'=16] {'col'}, use_global_device_ids=true, to_apply=%add | all-reduce | flops 512 | bytes 2048
  108.1 0.0 copy-done.4
  108.1 0.7 fusion.10
  112.0 20.5 %all-gather.2 = bf16[8,1,128]{2,1,0:T(2,128)(2,1)S(1)} all-gather(bf16[1,1,128]{2,1,0:T(2,128)(2,1)S(1)} %get-tuple-element.7), channel_id=1, replica_groups=mesh['tensor'=4,'row'=8,'col'=16] {'row'}, dimensions={0}, use_global_device_ids=true | all-gather | bytes 2304 | tf_op jit(solution)/shard_map/all_gather | solution.py:25
  132.5 0.0 all-gather.10.cloned.1.call-done
  132.5 1.5 fusion.3
  134.0 54.9 %all-gather.8.cloned.1.call-done = bf16[1024,1024]{1,0:T(8,128)(2,1)} async-done(((bf16[128,1024]{1,0:T(8,128)(2,1)}), bf16[1024,1024]{1,0:T(8,128)(2,1)}) %all-gather.8.cloned.1.call-update) | async-done | bytes 2097168 | tf_op jit(solution)/shard_map/all_gather | solution.py:24
  188.9 2.2 fusion
  191.2 0.0 copy-done.1
  191.2 0.0 copy-start.3
  191.2 8.2 %fusion.9 = (f32[512]{0:T(512)S(1)}, f32[1024]{0:T(1024)S(1)}, bf16[1024,512]{1,0:T(8,128)(2,1)S(1)}) fusion(f32[]{:T(128)S(6)} %mul.157, f32[]{:T(128)} %bitcast.8, f32[]{:T(128)S(6)} %mul.152, f32[]{:T(128)} %bitcast.7, f32[]{:T(128)S(6)} %mul.147, f32[]{:T(128)} %bitcast.6, f32[]{:T(128)S(6)} %mul.142, f32[]{:T(128)} %bitcast.5, f32[]{:T(128)S(6)} %mul.137, ...), kind=kOutput, calls=%fused_computation.20 | convolution fusion | flops 1085798912 | bytes 4212776 | tf_op jit(solution)/shard_map/dot_general | solution.py:33
  199.4 0.0 copy-start.6
  199.4 1.0 copy-done.6
  200.4 0.0 copy-done.3
  200.4 2.6 fusion.2
  203.0 0.0 reduce-scatter.3.cloned.1.call-update
  203.0 0.0 reduce-scatter.5.cloned.1.call-start
  203.1 4.5 %fusion.5 = bf16[512,1024]{1,0:T(8,128)(2,1)} fusion(bf16[512,1024]{1,0:T(8,128)(2,1)} %all-gather.10.cloned.1.call-done, bf16[1024,1024]{1,0:T(8,128)(2,1)} %all-gather.8.cloned.1.call-done, f32[512]{0:T(512)S(1)} %get-tuple-element.5, bf16[1024,512]{1,0:T(8,128)(2,1)} %copy-done.6), kind=kOutput, calls=%fused_computation.10 | convolution fusion | flops 1075838976 | bytes 5244928 | tf_op jit(solution)/shard_map/dot_general | solution.py:53
  207.5 0.0 reduce-scatter.5.cloned.1.call-update
  207.5 0.0 all-gather.14.cloned.1.call-start
  207.6 64.8 %reduce-scatter.3.cloned.1.call-done = bf16[128,1024]{1,0:T(8,128)(2,1)} async-done(((bf16[1024,1024]{1,0:T(8,128)(2,1)}), bf16[128,1024]{1,0:T(8,128)(2,1)}) %reduce-scatter.3.cloned.1.call-update) | async-done | bytes 262160 | tf_op jit(solution)/shard_map/reduce_scatter | solution.py:65
  272.4 1.8 convert_element_type.59
  274.1 89.8 %reduce-scatter.5.cloned.1.call-done = bf16[32,1024]{1,0:T(8,128)(2,1)} async-done(((bf16[512,1024]{1,0:T(8,128)(2,1)}), bf16[32,1024]{1,0:T(8,128)(2,1)}) %reduce-scatter.5.cloned.1.call-update) | async-done | bytes 65552 | tf_op jit(solution)/shard_map/reduce_scatter | solution.py:56
  363.9 1.6 add_dynamic-update-slice_fusion
  365.5 1.8 convert_element_type.63
  367.2 0.0 all-gather.14.cloned.1.call-update
  367.3 54.8 %all-gather.14.cloned.1.call-done = bf16[512,1024]{1,0:T(8,128)(2,1)} async-done(((bf16[128,1024]{1,0:T(8,128)(2,1)}), bf16[512,1024]{1,0:T(8,128)(2,1)}) %all-gather.14.cloned.1.call-update) | async-done | bytes 1048592 | tf_op jit(solution)/shard_map/all_gather | solution.py:8
  422.0 1.4 reduce_sum.65
  423.5 1.9 convolution_convert_fusion
  (7 shorter events, 0.0 us)
Async XLA Ops:
  6.5 1.9 copy-start
  6.5 66.1 %copy-start.5 = (s32[128]{0:T(128)S(1)}, s32[128]{0:T(128)}, u32[]{:S(2)}) copy-start(s32[128]{0:T(128)} %param.6) | copy-start | bytes 1540
  6.5 101.6 %copy-start.4 = (f32[5]{0:T(128)S(1)}, f32[5]{0:T(128)}, u32[]{:S(2)}) copy-start(f32[5]{0:T(128)} %param.7) | copy-start | bytes 64
  6.5 63.2 %all-gather.12.cloned.1.call-start = ((), (), s32[]{:S(2)}) async-start(), calls=%async_computation.6 | async-start | bytes 1310720 | tf_op jit(solution)/shard_map/all_gather | solution.py:8
  10.7 121.8 %all-gather.10.cloned.1.call-start = ((), (), s32[]{:S(2)}) async-start(), calls=%async_computation.3 | async-start | bytes 1114112 | tf_op jit(solution)/shard_map/all_gather | solution.py:28
  71.2 0.8 copy-start.2
  71.9 117.0 %all-gather.8.cloned.1.call-start = ((), (), s32[]{:S(2)}) async-start(), calls=%async_computation.2 | async-start | bytes 2359296 | tf_op jit(solution)/shard_map/all_gather | solution.py:24
  72.6 199.7 %reduce-scatter.3.cloned.1.call-start = ((), (), s32[]{:S(2)}) async-start(), calls=%async_computation.4 | async-start | bytes 2359296 | tf_op jit(solution)/shard_map/reduce_scatter | solution.py:65
  188.9 2.2 copy-start.1
  191.2 9.3 %copy-start.3 = (bf16[512,1024]{1,0:T(8,128)(2,1)S(1)}, bf16[512,1024]{1,0:T(8,128)(2,1)}, u32[]{:S(2)}) copy-start(bf16[512,1024]{1,0:T(8,128)(2,1)} %all-gather.10.cloned.1.call-done) | copy-start | bytes 3145732
  199.4 1.0 copy-start.6
  203.0 160.9 %reduce-scatter.5.cloned.1.call-start = ((), (), s32[]{:S(2)}) async-start(), calls=%async_computation.5 | async-start | bytes 1114112 | tf_op jit(solution)/shard_map/reduce_scatter | solution.py:56
  207.5 214.5 %all-gather.14.cloned.1.call-start = ((), (), s32[]{:S(2)}) async-start(), calls=%async_computation.7 | async-start | bytes 1310720 | tf_op jit(solution)/shard_map/all_gather | solution.py:8
Sparse Core Ops, SparseCore 0:
  10.9 58.8 all-gather.11
  72.7 47.5 all-gather.9
  122.4 66.4 all-gather.7
  203.1 69.1 reduce-scatter.2
  276.3 87.5 reduce-scatter.4
  367.4 54.6 all-gather.13
